TPU v7x, 32 devices: a whole 2x2x4 slice. The times are simulated.
32 devices in a mesh: seq: 16 (over z, y, core), req: 2 (over x).
Axes of the slice: x: 2, y: 2, z: 4, core: 2. Of those that a mesh axis runs over, the one named last changes fastest.
Arguments:
- hidden_in: bfloat16 [32, 4, 2048], P('req'), may hold values from -6 to 6
- attn_gain: float32 [2048], replicated, may hold values from 0.5 to 1.5
- q_gain: float32 [256], replicated, may hold values from 0.5 to 1.5
- k_gain: float32 [256], replicated, may hold values from 0.5 to 1.5
- post_attn_gain: float32 [2048], replicated, may hold values from 0.5 to 1.5
- ffn_gain: float32 [2048], replicated, may hold values from 0.5 to 1.5
- post_ffn_gain: float32 [2048], replicated, may hold values from 0.5 to 1.5
- w_qkv: bfloat16 [2048, 3072], P('seq', 'req'), may hold values from -0.125 to 0.125
- w_out: bfloat16 [2048, 2048], P('seq', 'req'), may hold values from -0.125 to 0.125
- w_gate: bfloat16 [2048, 8192], P('req', 'seq'), may hold values from -0.125 to 0.125
- w_up: bfloat16 [2048, 8192], P('req', 'seq'), may hold values from -0.125 to 0.125
- w_down: bfloat16 [8192, 2048], P('seq', 'req'), may hold values from -0.0625 to 0.0625
- prompt_keys: bfloat16 [4, 2048, 512], P('req', 'seq')
- prompt_values: bfloat16 [4, 2048, 512], P('req', 'seq'), may hold values from -6 to 6
- tail_keys: bfloat16 [2, 4096, 512], P('req', 'seq')
- tail_values: bfloat16 [2, 4096, 512], P('req', 'seq'), may hold values from -6 to 6
- group_of: int32 [32], P('req'), may hold values from 0 to 3, as said below
- prompt_lengths: int32 [4], P('req'), may hold values from 1 to 2048
- tail_lengths: int32 [32], P('req'), may hold values from 1 to 256
- page_table: int32 [2, 256], P('req'), may hold values from 0 to 255, each once within a row
Outputs:
- layer_out: bfloat16 [32, 4, 2048], P('req')
Inputs may be any that keep to these rules, and one draw needn't show every extreme that they name: `group_of`: request i belongs to one of the 2 groups i // 16 * 2 to i // 16 * 2 + 1 of its own block of requests. `page_table`: each row lists every pool page of its index of req once; entry j * 16 + p is the pool page of page p of the j-th request of that block.
All inputs are finite; a program needn't handle non-finite values.
Results may differ from a plain program's by a relative error of at most 0.012.
The roundings to bfloat16 on the way count: a program that leaves them out, or rounds other values in their place, can miss the bound.
Values may be sent and summed in bfloat16 or wider, within the bound.
No kernel may reach another device: no remote copies, remote signals or barrier semaphores. Data moves between devices by JAX's collectives and lax.ppermute only.
A program may use at most 128 MiB of HBM per device.

v0:
```python
import functools

import jax
import jax.numpy as jnp
from jax import lax
from jax.experimental import pallas as pl
from jax.experimental.pallas import tpu as pltpu
from jax.sharding import PartitionSpec as P

D = 2048
H = 8
KV = 2
HD = 256
PAGE = 16
QKV = 3072


EPSILON = 1e-06
NEGATIVE = -1e30
LINK_SCALE = 512.0


def normalize(values):
    return values * lax.rsqrt(jnp.mean(values * values, axis=-1, keepdims=True) + EPSILON)


def split_three(values):
    high = values.astype(jnp.bfloat16)
    rest = values - high.astype(jnp.float32)
    middle = rest.astype(jnp.bfloat16)
    low = (rest - middle.astype(jnp.float32)).astype(jnp.bfloat16)
    return jnp.stack([high, middle, low])


def exchange(blocks, axes, groups=None):
    return lax.all_to_all(
        blocks, axes, split_axis=0, concat_axis=0, tiled=True, axis_index_groups=groups
    )


def tie(*arrays):
    return lax.optimization_barrier(arrays)


def spread(block, copies):
    return jnp.broadcast_to(block[None], (copies,) + block.shape)


def gather_rows(rows, count):
    return exchange(spread(rows, count), "seq").reshape(count * rows.shape[0], rows.shape[1])


def call(
    kernel, name, out_shape, *operands, scratch=(), hbm_from=None, out_space=pltpu.VMEM, limit=16
):
    in_specs = [pl.BlockSpec(memory_space=pltpu.SMEM)]
    for i in range(1, len(operands)):
        space = pltpu.HBM if hbm_from is not None and i >= hbm_from else pltpu.VMEM
        in_specs.append(pl.BlockSpec(memory_space=space))
    return pl.pallas_call(
        kernel,
        name=name,
        out_shape=out_shape,
        in_specs=in_specs,
        out_specs=jax.tree.map(lambda _: pl.BlockSpec(memory_space=out_space), out_shape),
        scratch_shapes=scratch,
        compiler_params=pltpu.CompilerParams(vmem_limit_bytes=limit * 1024 * 1024),
    )(*operands)


def norm_columns_kernel(where_ref, hidden_ref, gain_ref, out_ref):
    columns = out_ref.shape[1]
    hidden = hidden_ref[...].astype(jnp.float32)
    scale = lax.rsqrt(jnp.mean(hidden * hidden, axis=-1, keepdims=True) + EPSILON)
    cols = pl.ds(pl.multiple_of(where_ref[0] * columns, columns), columns)
    normed = hidden_ref[:, :, cols].astype(jnp.float32) * scale * gain_ref[:, cols]
    out_ref[...] = normed.reshape(out_ref.shape).astype(jnp.bfloat16)


def head_norm_kernel(where_ref, projected_ref, gains_ref, q_ref, k_ref, v_ref):
    width = projected_ref.shape[2]
    copies, rows, _ = q_ref.shape
    fill = jnp.zeros((k_ref.shape[0] - rows, HD), jnp.float32)
    for head in range(H + 2 * KV):
        half, first = divmod(head * HD, width)
        values = normalize(projected_ref[half, :, first : first + HD])
        if head < H:
            values = (values * gains_ref[0:1, :]).astype(jnp.bfloat16)
            for i in range(copies):
                q_ref[i, :, head * HD : (head + 1) * HD] = values
        else:
            if head < H + KV:
                values = values * gains_ref[1:2, :]
            values = values.astype(jnp.bfloat16).astype(jnp.float32)
            target, slot = (k_ref, head - H) if head < H + KV else (v_ref, head - H - KV)
            target[:, slot * HD : (slot + 1) * HD] = jnp.concatenate([values, fill])


def dot_last(a, b):
    return lax.dot_general(a, b, (((1,), (1,)), ((), ())), preferred_element_type=jnp.float32)


def block_kernel(
    step_count,
    where_ref,
    q_ref,
    live_ref,
    new_k_ref,
    new_v_ref,
    keys_ref,
    values_ref,
    out_ref,
):
    copies, steps, _ = q_ref.shape
    tokens = copies * steps
    columns = out_ref.shape[2]
    group = H // KV
    queries = q_ref[...].reshape(tokens, H * HD)
    live = jnp.concatenate([live_ref[...]] * group) > 0.5
    first_token = where_ref[0] * step_count
    shape = (group * tokens, new_k_ref.shape[0])
    step = lax.broadcasted_iota(jnp.int32, shape, 0) % tokens - first_token
    new_index = lax.broadcasted_iota(jnp.int32, shape, 1)
    new_live = (step >= new_index) & (step < step_count)
    for kv in range(KV):
        span = slice(kv * HD, (kv + 1) * HD)
        q = jnp.concatenate(
            [queries[:, (kv * group + g) * HD : (kv * group + g + 1) * HD] for g in range(group)]
        )
        scores = jnp.where(live, dot_last(q, keys_ref[:, span]), NEGATIVE)
        top = jnp.max(scores, axis=1, keepdims=True)
        probs = jnp.where(live, jnp.exp(scores - top), 0.0)
        total = jnp.sum(probs, axis=1, keepdims=True)
        accum = jnp.dot(
            probs.astype(jnp.bfloat16), values_ref[:, span], preferred_element_type=jnp.float32
        )
        new_scores = dot_last(q, new_k_ref[:, span].astype(jnp.bfloat16))
        new_scores = jnp.where(new_live, new_scores, NEGATIVE)
        both = jnp.maximum(top, jnp.max(new_scores, axis=1, keepdims=True))
        carried = jnp.exp(top - both)
        new_probs = jnp.where(new_live, jnp.exp(new_scores - both), 0.0)
        total = total * carried + jnp.sum(new_probs, axis=1, keepdims=True)
        accum = accum * carried
        for u in range(step_count):
            accum = accum + new_probs[:, u : u + 1] * new_v_ref[u : u + 1, span]
        sent = accum.astype(jnp.bfloat16)
        parts = []
        for value in (both, total):
            for _ in range(3):
                part = value.astype(jnp.bfloat16).astype(jnp.float32)
                parts.append(part)
                value = value - part
        lane = lax.broadcasted_iota(jnp.int32, (group * tokens, 128), 1)
        wide = jnp.zeros((group * tokens, 128), jnp.float32)
        for i, part in enumerate(parts):
            wide = jnp.where(lane == i, part, wide)
        turned = jnp.transpose(wide)[:16].astype(jnp.bfloat16)
        for g in range(group):
            pair = turned[:, g // 2 * 128 : (g // 2 + 1) * 128]
            for part in range(HD // columns):
                target = (kv * group + g) * (HD // columns) + part
                out_ref[target, :tokens, :] = sent[
                    g * tokens : (g + 1) * tokens, part * columns : (part + 1) * columns
                ]
                out_ref[target, tokens:, :] = pair


def out_kernel(req_count, where_ref, got_ref, *refs):
    w_refs = refs[:req_count]
    out_ref, turned_ref = refs[req_count:]
    blocks = got_ref.shape[0]
    copies, steps, _ = out_ref.shape
    tokens = copies * steps
    columns = got_ref.shape[2]
    head = where_ref[0] * columns // HD
    stats = got_ref[:, tokens:, :].astype(jnp.float32)
    tops = stats[:, 0, :] + stats[:, 1, :] + stats[:, 2, :]
    totals = stats[:, 3, :] + stats[:, 4, :] + stats[:, 5, :]
    rest = jnp.zeros((128 - 2 * blocks, 128), jnp.float32)
    turned_ref[...] = jnp.transpose(jnp.concatenate([tops, totals, rest]))
    mine = turned_ref[pl.ds(pl.multiple_of(head % 2 * tokens, tokens), tokens), :]
    tops = mine[:, :blocks]
    highest = jnp.max(tops, axis=1, keepdims=True)
    weights = jnp.exp(tops - highest)
    denominator = jnp.sum(mine[:, blocks : 2 * blocks] * weights, axis=1, keepdims=True)
    numerator = jnp.zeros((tokens, columns), jnp.float32)
    for b in range(blocks):
        numerator = numerator + got_ref[b, :tokens, :].astype(jnp.float32) * weights[:, b : b + 1]
    attention = (numerator / denominator).astype(jnp.bfloat16)
    for j, w_ref in enumerate(w_refs):
        width = w_ref.shape[1]
        part = jnp.dot(attention, w_ref[...], preferred_element_type=jnp.float32)
        part = part.astype(jnp.bfloat16)
        for i in range(copies):
            out_ref[i, :, j * width : (j + 1) * width] = part[i * steps : (i + 1) * steps]


def summed(req_count, where_ref, got_ref):
    width = got_ref.shape[2] // req_count
    blocks = []
    for i in range(req_count):
        j = lax.rem(where_ref[1] - i + req_count, req_count)
        cols = pl.ds(pl.multiple_of(j * width, width), width)
        blocks.append(jnp.sum(got_ref[:, :, cols].astype(jnp.float32), axis=0))
    return jnp.concatenate(blocks, axis=1)


def residual_kernel(
    req_count, where_ref, got_ref, hidden_ref, post_gain_ref, ffn_gain_ref, out_ref, residual_ref
):
    attn_out = summed(req_count, where_ref, got_ref)
    residual = hidden_ref[...].astype(jnp.float32) + normalize(attn_out) * post_gain_ref[...]
    residual_ref[...] = residual
    ffn_in = (normalize(residual) * ffn_gain_ref[...]).astype(jnp.bfloat16)
    for i in range(out_ref.shape[0]):
        out_ref[i] = ffn_in


def last_kernel(req_count, where_ref, got_ref, residual_ref, gain_ref, out_ref):
    down_out = summed(req_count, where_ref, got_ref)
    layer = (residual_ref[...] + normalize(down_out) * gain_ref[...]).astype(jnp.bfloat16)
    for i in range(out_ref.shape[0]):
        out_ref[i] = layer


def ffn_kernel(req_count, where_ref, x_ref, *refs):
    count = req_count + 2
    w_refs, out_ref, x_held, parts_ref = refs[:count], *refs[count : count + 3]
    held, sem_ref = refs[count + 3 : -1], refs[-1]
    gate_rows, width = w_refs[0].shape
    down_rows, down_width = w_refs[2].shape
    load_x = pltpu.make_async_copy(x_ref, x_held, sem_ref.at[3 * req_count])
    load_x.start()
    x_ref = x_held
    copies = []

    def load(source, target):
        copies.append(pltpu.make_async_copy(source, target, sem_ref.at[len(copies)]))
        copies[-1].start()

    for i in range(3):
        load(w_refs[i], held[i])
    packed_rows = 2 * gate_rows + down_rows * (down_width // width)
    spans = [(0, gate_rows), (gate_rows, gate_rows), (2 * gate_rows, packed_rows - 2 * gate_rows)]
    for j in range(3, count):
        for first, rows in spans:
            load(w_refs[j].at[pl.ds(first, rows), :], held[j].at[pl.ds(first, rows), :])
    blocks, steps, _ = x_ref.shape
    tokens = blocks * steps
    load_x.wait()
    gate_out = up_out = None
    for j in range(req_count):
        first = lax.rem(where_ref[1] - j + req_count, req_count) * gate_rows
        cols = pl.ds(pl.multiple_of(first, gate_rows), gate_rows)
        part = x_ref[:, :, cols].reshape(tokens, gate_rows)
        copies[3 * j].wait()
        gate_w = held[0][...] if j == 0 else held[j + 2][:gate_rows, :]
        gate = jnp.dot(part, gate_w, preferred_element_type=jnp.float32)
        copies[3 * j + 1].wait()
        up_w = held[1][...] if j == 0 else held[j + 2][gate_rows : 2 * gate_rows, :]
        up = jnp.dot(part, up_w, preferred_element_type=jnp.float32)
        gate_out = gate if j == 0 else gate_out + gate
        up_out = up if j == 0 else up_out + up
    activated = (jax.nn.gelu(gate_out, approximate=True) * up_out).astype(jnp.bfloat16)
    sends = []
    for j in range(req_count):
        copies[3 * j + 2].wait()
        for piece in range(down_width // width):
            if j == 0:
                down_w = held[2][:, piece * width : (piece + 1) * width]
            else:
                row = 2 * gate_rows + piece * down_rows
                down_w = held[j + 2][row : row + down_rows, :]
            part = jnp.dot(activated, down_w, preferred_element_type=jnp.float32)
            part = part.astype(jnp.bfloat16)
            index = j * (down_width // width) + piece
            for i in range(blocks):
                parts_ref[index, i] = part[i * steps : (i + 1) * steps]
            sends.append(
                pltpu.make_async_copy(
                    parts_ref.at[index],
                    out_ref.at[:, :, pl.ds(index * width, width)],
                    sem_ref.at[3 * req_count + 1 + index],
                )
            )
            sends[-1].start()
    for send in sends:
        send.wait()


def live_rows(
    seq_index, prompt_shape, pool_rows, group_of, prompt_lengths, tail_lengths, page_table
):
    group_count, prompt_span = prompt_shape
    rows_req = group_of.shape[0]
    member = (group_of % group_count)[:, None] == jnp.arange(group_count, dtype=jnp.int32)[None, :]
    prompt_pos = seq_index * prompt_span + jnp.arange(prompt_span, dtype=jnp.int32)
    prompt_live = prompt_pos[None, :] < prompt_lengths[:, None]
    prompt_mask = (member[:, :, None] & prompt_live[None, :, :]).reshape(
        rows_req, group_count * prompt_span
    )
    slot_count = pool_rows // PAGE
    table_row = page_table[0]
    table_len = table_row.shape[0]
    tail_pages = table_len // rows_req
    slot_ids = seq_index * slot_count + jnp.arange(slot_count, dtype=jnp.int32)
    matches = table_row[None, :] == slot_ids[:, None]
    entries = jnp.sum(
        jnp.where(matches, jnp.arange(table_len, dtype=jnp.int32)[None, :], 0), axis=1
    )
    owners = jnp.repeat(entries // tail_pages, PAGE)
    tail_pos = jnp.repeat(entries % tail_pages, PAGE) * PAGE + jnp.tile(
        jnp.arange(PAGE, dtype=jnp.int32), slot_count
    )
    tail_mask = (owners[None, :] == jnp.arange(rows_req, dtype=jnp.int32)[:, None]) & (
        tail_pos[None, :] < tail_lengths[:, None]
    )
    return jnp.concatenate([prompt_mask, tail_mask], axis=1)


def general_attention(
    seq_index,
    seq_count,
    rows_req,
    step_count,
    out_rows,
    projected,
    q_gain,
    k_gain,
    live,
    prompt_keys,
    prompt_values,
    tail_keys,
    tail_values,
):
    group_size = H // KV
    share = projected.shape[0]
    tokens = rows_req * step_count
    heads = normalize(projected.reshape(share, QKV // HD, HD))
    gains = jnp.concatenate(
        [
            jnp.broadcast_to(q_gain, (H, HD)),
            jnp.broadcast_to(k_gain, (KV, HD)),
            jnp.ones((KV, HD), jnp.float32),
        ]
    )
    mine = (heads * gains).astype(jnp.bfloat16).reshape(share, QKV)
    qkv = gather_rows(mine, seq_count)
    queries = qkv[:, : H * HD]
    keys_new = qkv[:, H * HD : (H + KV) * HD]
    values_new = qkv[:, (H + KV) * HD :]

    query_groups = queries.reshape(rows_req, step_count, KV, group_size, HD)
    mask = live[:, None, None, None, :]
    keys = jnp.concatenate([prompt_keys, tail_keys]).reshape(-1, KV, HD)
    values = jnp.concatenate([prompt_values, tail_values]).reshape(-1, KV, HD)
    scores = jnp.einsum("rskgd,pkd->rskgp", query_groups, keys, preferred_element_type=jnp.float32)
    scores = jnp.where(mask, scores, NEGATIVE)
    block_top = jnp.max(scores, axis=4)
    probs = jnp.where(mask, jnp.exp(scores - block_top[..., None]), 0.0)
    block_total = jnp.sum(probs, axis=4)
    block_accum = jnp.einsum(
        "rskgp,pkd->rskgd",
        probs.astype(jnp.bfloat16),
        values,
        preferred_element_type=jnp.float32,
    )

    stats = split_three(jnp.stack([block_top, block_total])).reshape(6, tokens, H)
    per_head = seq_count // H
    stats = jnp.repeat(stats.transpose(2, 0, 1).reshape(H, -1, out_rows), per_head, axis=0)
    accum_blocks = (
        block_accum.astype(jnp.bfloat16).reshape(tokens, seq_count, out_rows).transpose(1, 0, 2)
    )
    got = exchange(jnp.concatenate([accum_blocks, stats], axis=1), "seq")
    got_accum = got[:, :tokens].astype(jnp.float32)
    got_stats = got[:, tokens:].astype(jnp.float32).reshape(seq_count, 2 * 3, tokens)
    got_top = got_stats[:, 0] + got_stats[:, 2] + got_stats[:, 4]
    got_total = got_stats[:, 1] + got_stats[:, 3] + got_stats[:, 5]

    first_col = seq_index * out_rows
    head = first_col // HD
    kv_head = head // group_size
    head_queries = lax.dynamic_slice_in_dim(queries, head * HD, HD, 1)
    head_keys = lax.dynamic_slice_in_dim(keys_new, kv_head * HD, HD, 1)
    head_values = lax.dynamic_slice_in_dim(
        values_new, kv_head * HD + first_col % HD, out_rows, 1
    ).astype(jnp.float32)
    new_scores = jnp.dot(head_queries, head_keys.T, preferred_element_type=jnp.float32)
    token_ids = jnp.arange(tokens, dtype=jnp.int32)
    causal = (token_ids[:, None] // step_count == token_ids[None, :] // step_count) & (
        token_ids[:, None] >= token_ids[None, :]
    )
    new_scores = jnp.where(causal, new_scores, NEGATIVE)
    highest = jnp.maximum(jnp.max(got_top, axis=0), jnp.max(new_scores, axis=1))
    weights = jnp.exp(got_top - highest[None])
    new_probs = jnp.where(causal, jnp.exp(new_scores - highest[:, None]), 0.0)
    denominator = jnp.sum(got_total * weights, axis=0) + jnp.sum(new_probs, axis=1)
    numerator = jnp.sum(got_accum * weights[..., None], axis=0) + jnp.dot(
        new_probs, head_values, precision=lax.Precision.HIGHEST
    )
    return (numerator / denominator[:, None]).astype(jnp.bfloat16)


def on_device(
    req_count,
    seq_count,
    hidden_in,
    attn_gain,
    q_gain,
    k_gain,
    post_attn_gain,
    ffn_gain,
    post_ffn_gain,
    w_qkv,
    w_out,
    w_gate,
    w_up,
    w_down,
    prompt_keys,
    prompt_values,
    tail_keys,
    tail_values,
    group_of,
    prompt_lengths,
    tail_lengths,
    page_table,
):
    seq_index = lax.axis_index("seq")
    req_index = lax.axis_index("req")
    rows_req, step_count, _ = hidden_in.shape
    group_size = H // KV
    tokens = rows_req * step_count
    share = tokens // seq_count

    def shifted(values):
        return [values] + [
            lax.ppermute(values, "req", [(i, (i + j) % req_count) for i in range(req_count)])
            for j in range(1, req_count)
        ]

    where = jnp.stack([seq_index, req_index]).astype(jnp.int32)
    in_rows = w_qkv.shape[0]
    out_rows = w_out.shape[0]
    if in_rows % 128 == 0:
        normed_cols = call(
            norm_columns_kernel,
            "norm_columns",
            jax.ShapeDtypeStruct((tokens, in_rows), jnp.bfloat16),
            seq_index.astype(jnp.int32).reshape(1),
            hidden_in,
            attn_gain.reshape(1, D),
            limit=56,
        )
    else:
        normed = (normalize(hidden_in.astype(jnp.float32)) * attn_gain).astype(jnp.bfloat16)
        normed_cols = lax.dynamic_slice_in_dim(normed, seq_index * in_rows, in_rows, 2)
        normed_cols = normed_cols.reshape(tokens, in_rows)
    normed_all = lax.all_gather(normed_cols, "req", axis=0, tiled=True)
    out_blocks = shifted(w_out)
    width = w_gate.shape[1]
    pieces = [w_down[:, c : c + width] for c in range(0, w_down.shape[1], width)]
    packed = shifted(jnp.concatenate([w_gate, w_up] + pieces))[1:]

    qkv_part = jnp.dot(normed_all, w_qkv, preferred_element_type=jnp.float32)
    qkv_cols = w_qkv.shape[1]
    qkv_blocks = (
        (qkv_part * LINK_SCALE)
        .astype(jnp.float16)
        .reshape(req_count * seq_count, share, qkv_cols)
    )
    qkv_got = exchange(qkv_blocks, ("req", "seq"))
    qkv_got = qkv_got.reshape(req_count, seq_count, share, qkv_cols)
    projected = jnp.sum(qkv_got.astype(jnp.float32), axis=1) * (1.0 / LINK_SCALE)
    live = live_rows(
        seq_index, prompt_keys.shape[:2], tail_keys.shape[1], group_of, prompt_lengths,
        tail_lengths, page_table,
    )
    caches = [
        array.reshape(-1, KV * HD) for array in (prompt_keys, prompt_values, tail_keys, tail_values)
    ]
    direct = share == step_count and out_rows % 128 == 0 and tokens == 64 and qkv_cols % HD == 0
    if direct:
        q_blocks, new_keys, new_values = call(
            head_norm_kernel,
            "head_norm",
            (
                jax.ShapeDtypeStruct((seq_count, share, H * HD), jnp.bfloat16),
                jax.ShapeDtypeStruct((8, KV * HD), jnp.float32),
                jax.ShapeDtypeStruct((8, KV * HD), jnp.float32),
            ),
            where,
            projected,
            jnp.stack([q_gain, k_gain]),
        )
        q_got, out_blocks = tie(exchange(q_blocks, "seq"), out_blocks)
        live = jnp.repeat(live.astype(jnp.float32), step_count, axis=0)
        sent = call(
            functools.partial(block_kernel, step_count),
            "block_attention",
            jax.ShapeDtypeStruct((seq_count, tokens + 16, out_rows), jnp.bfloat16),
            where,
            q_got,
            live,
            new_keys,
            new_values,
            jnp.concatenate([caches[0], caches[2]]),
            jnp.concatenate([caches[1], caches[3]]),
        )
        got = exchange(sent, "seq")
        out_part = call(
            functools.partial(out_kernel, req_count),
            "combine_out",
            jax.ShapeDtypeStruct((seq_count, share, D), jnp.bfloat16),
            where,
            got,
            *out_blocks,
            scratch=[pltpu.VMEM((128, 128), jnp.float32)],
        )
    else:
        projected = projected.transpose(1, 0, 2).reshape(share, QKV)
        attention_cols = general_attention(
            seq_index, seq_count, rows_req, step_count, out_rows, projected, q_gain, k_gain,
            live, *caches,
        )
        out_part = jnp.concatenate(
            [jnp.dot(attention_cols, w, preferred_element_type=jnp.float32) for w in out_blocks],
            axis=1,
        )
        out_part = out_part.astype(jnp.bfloat16).reshape(seq_count, share, D)
    hidden_mine = lax.dynamic_index_in_dim(
        hidden_in.reshape(seq_count, share, D), seq_index, 0, keepdims=False
    )
    ffn_blocks, residual = call(
        functools.partial(residual_kernel, req_count),
        "residual_norms",
        (
            jax.ShapeDtypeStruct((seq_count, share, D), jnp.bfloat16),
            jax.ShapeDtypeStruct((share, D), jnp.float32),
        ),
        where,
        exchange(out_part, "seq"),
        hidden_mine,
        post_attn_gain.reshape(1, D),
        ffn_gain.reshape(1, D),
    )
    held = [w_gate, w_up, w_down] + list(packed)
    down_part = call(
        functools.partial(ffn_kernel, req_count),
        "feed_forward",
        jax.ShapeDtypeStruct((seq_count, share, D), jnp.bfloat16),
        where,
        exchange(ffn_blocks, "seq"),
        *held,
        scratch=[
            pltpu.VMEM((seq_count, share, D), jnp.bfloat16),
            pltpu.VMEM((D // width, seq_count, share, width), jnp.bfloat16),
        ]
        + [pltpu.VMEM(w.shape, w.dtype) for w in held]
        + [pltpu.SemaphoreType.DMA((3 * req_count + 1 + D // width,))],
        hbm_from=1,
        out_space=pltpu.HBM,
        limit=56,
    )
    layer_blocks = call(
        functools.partial(last_kernel, req_count),
        "last_norm",
        jax.ShapeDtypeStruct((seq_count, share, D), jnp.bfloat16),
        where,
        exchange(down_part, "seq"),
        residual,
        post_ffn_gain.reshape(1, D),
    )
    return exchange(layer_blocks, "seq").reshape(rows_req, step_count, D)


def solution(mesh):
    return jax.shard_map(
        functools.partial(on_device, mesh.shape["req"], mesh.shape["seq"]),
        mesh=mesh,
        in_specs=(
            P("req", None, None),
            P(),
            P(),
            P(),
            P(),
            P(),
            P(),
            P("seq", "req"),
            P("seq", "req"),
            P("req", "seq"),
            P("req", "seq"),
            P("seq", "req"),
            P("req", "seq", None),
            P("req", "seq", None),
            P("req", "seq", None),
            P("req", "seq", None),
            P("req"),
            P("req"),
            P("req"),
            P("req", None),
        ),
        out_specs=P("req", None, None),
        check_vma=False,
    )
```

profile of v0, /device:TPU:0, one launch (start us, length us, event | category | flops | bytes accessed | tf_op | source)
XLA Modules:
  0.0 127.6 jit_solution(1149682770308263314)
XLA Ops:
  0.0 0.0 copy-start
  0.0 3.0 %collective-permute-start = (bf16[128,1024]{1,0:T(8,128)(2,1)}, bf16[128,1024]{1,0:T(8,128)(2,1)S(1)}, u32[]{:S(2)}, u32[]{:S(2)}) collective-permute-start(bf16[128,1024]{1,0:T(8,128)(2,1)} %refs_0_.1), channel_id=1, source_target_pairs={{0,1},{1,0},{2,3},{3,2},{4,5},{5,4},{6,7},{7,6},{8,9},{9,8},{10,11... | collective-permute-start | bytes 786440 | tf_op jit(solution)/shard_map/ppermute | solution.py:438
  3.0 1.8 %norm_columns.1 = bf16[64,128]{1,0:T(8,128)(2,1)} custom-call(s32[1]{0:T(128)} %bitcast.where_ref, bf16[16,4,2048]{2,1,0:T(4,128)(2,1)} %hidden_ref.1, f32[1,2048]{1,0:T(1,128)} %bitcast.34), custom_call_target="tpu_custom_call" | custom-call | tf_op jit(solution)/shard_map/norm_columns/pallas_call | solution.py:60
  4.8 5.1 %all_gather.3 = bf16[128,128]{1,0:T(8,128)(2,1)S(1)} all-gather(bf16[64,128]{1,0:T(8,128)(2,1)} %norm_columns.1), channel_id=1, replica_groups=mesh['seq'=16,'req'=2] {'req'}, dimensions={0}, use_global_device_ids=true | all-gather | bytes 49152 | tf_op jit(solution)/shard_map/all_gather | solution.py:459
  9.9 0.0 copy-done
  9.9 0.3 fusion
  10.1 0.9 reshape.106
  11.0 6.1 %all-to-all-start = ((f16[32,4,1536]{2,1,0:T(4,128)(2,1)}), f16[32,4,1536]{2,1,0:T(4,128)(2,1)S(1)}, u32[]{:S(2)}, u32[]{:S(2)}) async-start(f16[32,4,1536]{2,1,0:T(4,128)(2,1)} %reshape.106), calls=%async_computation | async-start | bytes 786432 | tf_op jit(solution)/shard_map/all_to_all | solution.py:36
  17.1 0.0 copy-done.7
  17.2 0.1 fusion.4
  17.2 0.0 copy-done.8
  17.2 0.0 copy-start.10
  17.3 0.0 copy-start.11
  17.3 0.0 copy-start.12
  17.3 0.0 copy-start.14
  17.3 0.0 copy-start.15
  17.3 0.0 copy-start.13
  17.3 0.0 copy-start.9
  17.3 2.9 %pad_maximum_fusion = bf16[3072,512]{1,0:T(8,128)(2,1)} fusion(bf16[512,512]{1,0:T(8,128)(2,1)S(1)} %get-tuple-element.22, bf16[512,512]{1,0:T(8,128)(2,1)S(1)} %get-tuple-element.21, bf16[1024,512]{1,0:T(8,128)(2,1)} %refs_1_.1, bf16[1024,512]{1,0:T(8,128)(2,1)S(1)} %copy-done.8), kind=kLoop, calls=%fused_computation | loop fusion | flops 12582912 | bytes 6291456 | tf_op jit(solution)/shard_map/concatenate | solution.py:463
  20.2 1.8 %collective-permute-start.1 = (bf16[3072,512]{1,0:T(8,128)(2,1)}, bf16[3072,512]{1,0:T(8,128)(2,1)}, u32[]{:S(2)}, u32[]{:S(2)}) collective-permute-start(bf16[3072,512]{1,0:T(8,128)(2,1)} %pad_maximum_fusion), channel_id=1, source_target_pairs={{0,1},{1,0},{2,3},{3,2},{4,5},{5,4},{6,7},{7,6},{8,9},{9,8},{10,11... | collective-permute-start | bytes 9437192 | tf_op jit(solution)/shard_map/ppermute | solution.py:438
  22.0 0.1 pad_add_fusion.where_ref
  22.0 0.0 copy-done.10
  22.0 0.2 select_reduce_fusion
  22.2 0.0 copy-done.11
  22.3 0.0 copy-done.12
  22.3 0.0 copy-done.14
  22.3 0.1 iota_compare_fusion.1
  22.4 0.1 iota_add_fusion
  22.5 7.8 %all-to-all-done = f16[32,4,1536]{2,1,0:T(4,128)(2,1)S(1)} async-done(((f16[32,4,1536]{2,1,0:T(4,128)(2,1)}), f16[32,4,1536]{2,1,0:T(4,128)(2,1)S(1)}, u32[]{:S(2)}, u32[]{:S(2)}) %all-to-all-start) | async-done | bytes 393248 | tf_op jit(solution)/shard_map/all_to_all | solution.py:36
  30.3 0.2 convert_reduce_fusion
  30.4 1.4 %head_norm.1 = (bf16[16,4,2048]{2,1,0:T(4,128)(2,1)}, f32[8,512]{1,0:T(8,128)S(1)}, f32[8,512]{1,0:T(8,128)S(1)}) custom-call(s32[2]{0:T(128)S(1)} %pad_add_fusion.where_ref, f32[2,4,1536]{2,1,0:T(4,128)S(1)} %broadcast_multiply_fusion.projected_ref, f32[2,256]{1,0:T(2,128)S(1)} %pad_maximum_fusion.3.gains_ref), custom_call_target="tpu_custom_call" | custom-call | tf_op jit(solution)/shard_map/head_norm/pallas_call | solution.py:60
  31.8 3.5 %all-to-all-start.1 = ((bf16[16,4,2048]{2,1,0:T(4,128)(2,1)}), bf16[16,4,2048]{2,1,0:T(4,128)(2,1)S(1)}, u32[]{:S(2)}, u32[]{:S(2)}) async-start(bf16[16,4,2048]{2,1,0:T(4,128)(2,1)} %get-tuple-element.13), calls=%async_computation.1 | async-start | bytes 524288 | tf_op jit(solution)/shard_map/all_to_all | solution.py:36
  35.4 0.0 copy-done.15
  35.4 0.1 lt.51
  35.5 0.1 broadcast_in_dim.20
  35.5 0.1 eq.57
  35.6 0.1 add.52
  35.7 0.1 and.36
  35.8 0.0 copy-done.13
  35.8 0.1 fusion.1
  36.0 0.0 copy-start.5
  36.0 0.0 copy-start.6
  36.0 0.0 copy-done.9
  36.0 1.2 pad_maximum_fusion.1
  37.2 0.0 collective-permute-done.refs_1_
  37.2 8.2 %all-to-all-done.1.q_ref = bf16[16,4,2048]{2,1,0:T(4,128)(2,1)S(1)} async-done(((bf16[16,4,2048]{2,1,0:T(4,128)(2,1)}), bf16[16,4,2048]{2,1,0:T(4,128)(2,1)S(1)}, u32[]{:S(2)}, u32[]{:S(2)}) %all-to-all-start.1) | async-done | bytes 262176 | tf_op jit(solution)/shard_map/all_to_all | solution.py:36
  45.4 2.6 %block_attention.1 = bf16[16,80,128]{2,1,0:T(8,128)(2,1)S(1)} custom-call(s32[2]{0:T(128)S(1)} %pad_add_fusion.where_ref, bf16[16,4,2048]{2,1,0:T(4,128)(2,1)S(1)} %all-to-all-done.1.q_ref, f32[64,512]{1,0:T(8,128)S(1)} %reshape.107.live_ref, f32[8,512]{1,0:T(8,128)S(1)} %get-tuple-element.15.new_k_ref, f32[8,512]{1,0:T(8,128)S(1)} %get-tuple-element.16.new_v_ref, ...), custom_call_target="tpu_custom_call" | custom-call | tf_op jit(solution)/shard_map/block_attention/pallas_call | solution.py:60
  48.0 13.9 %all_to_all.35.got_ref = bf16[16,80,128]{2,1,0:T(8,128)(2,1)S(1)} all-to-all(bf16[16,80,128]{2,1,0:T(8,128)(2,1)S(1)} %block_attention.1), channel_id=1, replica_groups=mesh['seq'=16,'req'=2] {'seq'}, dimensions={0} | all-to-all | bytes 655360 | tf_op jit(solution)/shard_map/all_to_all | solution.py:36
  61.9 0.0 copy-done.1
  61.9 2.0 %combine_out.1 = bf16[16,4,2048]{2,1,0:T(4,128)(2,1)} custom-call(s32[2]{0:T(128)S(1)} %pad_add_fusion.where_ref, bf16[16,80,128]{2,1,0:T(8,128)(2,1)S(1)} %all_to_all.35.got_ref, bf16[128,1024]{1,0:T(8,128)(2,1)S(1)} %copy-done.1, bf16[128,1024]{1,0:T(8,128)(2,1)S(1)} %collective-permute-done.refs_1_), custom_call_target="tpu_custom_call" | custom-call | tf_op jit(solution)/shard_map/combine_out/pallas_call | solution.py:60
  63.9 3.5 %all-to-all-start.3 = ((bf16[16,4,2048]{2,1,0:T(4,128)(2,1)}), bf16[16,4,2048]{2,1,0:T(4,128)(2,1)S(1)}, u32[]{:S(2)}, u32[]{:S(2)}) async-start(bf16[16,4,2048]{2,1,0:T(4,128)(2,1)} %combine_out.1), calls=%async_computation.3 | async-start | bytes 524288 | tf_op jit(solution)/shard_map/all_to_all | solution.py:36
  67.5 0.7 dynamic-slice_bitcast_fusion.hidden_ref
  68.2 9.3 %all-to-all-done.3.got_ref = bf16[16,4,2048]{2,1,0:T(4,128)(2,1)S(1)} async-done(((bf16[16,4,2048]{2,1,0:T(4,128)(2,1)}), bf16[16,4,2048]{2,1,0:T(4,128)(2,1)S(1)}, u32[]{:S(2)}, u32[]{:S(2)}) %all-to-all-start.3) | async-done | bytes 262176 | tf_op jit(solution)/shard_map/all_to_all | solution.py:36
  77.5 0.0 copy-done.2
  77.5 0.0 copy-done.5
  77.5 0.9 residual_norms.1
  78.4 13.3 %all_to_all.36.x_ref = bf16[16,4,2048]{2,1,0:T(4,128)(2,1)} all-to-all(bf16[16,4,2048]{2,1,0:T(4,128)(2,1)S(1)} %get-tuple-element.19), channel_id=1, replica_groups=mesh['seq'=16,'req'=2] {'seq'}, dimensions={0} | all-to-all | bytes 524288 | tf_op jit(solution)/shard_map/all_to_all | solution.py:36
  91.7 1.1 collective-permute-done.1.refs_3_
  92.7 5.2 %feed_forward.1 = bf16[16,4,2048]{2,1,0:T(4,128)(2,1)} custom-call(s32[2]{0:T(128)} %copy-done.2, bf16[16,4,2048]{2,1,0:T(4,128)(2,1)} %all_to_all.36.x_ref, bf16[1024,512]{1,0:T(8,128)(2,1)} %refs_0_.2, bf16[1024,512]{1,0:T(8,128)(2,1)} %refs_1_.1, bf16[512,1024]{1,0:T(8,128)(2,1)} %refs_2_.1, bf16[3072,512]{1,0:T(8,128)(2,1)} %collective-permute-done.1.refs_3_), custom_call_target="tpu_custom_call" | custom-call | tf_op jit(solution)/shard_map/feed_forward/pallas_call | solution.py:60
  98.0 15.4 %all_to_all.37.got_ref = bf16[16,4,2048]{2,1,0:T(4,128)(2,1)S(1)} all-to-all(bf16[16,4,2048]{2,1,0:T(4,128)(2,1)} %feed_forward.1), channel_id=1, replica_groups=mesh['seq'=16,'req'=2] {'seq'}, dimensions={0} | all-to-all | bytes 524288 | tf_op jit(solution)/shard_map/all_to_all | solution.py:36
  113.3 0.0 copy-done.4
  113.3 0.8 last_norm.1
  114.1 12.8 %all_to_all.38 = bf16[16,4,2048]{2,1,0:T(4,128)(2,1)S(1)} all-to-all(bf16[16,4,2048]{2,1,0:T(4,128)(2,1)S(1)} %last_norm.1), channel_id=1, replica_groups=mesh['seq'=16,'req'=2] {'seq'}, dimensions={0} | all-to-all | bytes 524288 | tf_op jit(solution)/shard_map/all_to_all | solution.py:36
  126.9 0.7 copy.24
  (18 shorter events, 0.2 us)
Async XLA Ops:
  0.0 9.9 %copy-start = (bf16[128,1536]{1,0:T(8,128)(2,1)S(1)}, bf16[128,1536]{1,0:T(8,128)(2,1)}, u32[]{:S(2)}) copy-start(bf16[128,1536]{1,0:T(8,128)(2,1)} %param.27) | copy-start | bytes 1179652
  0.0 17.1 %copy-start.7 = (bf16[512,1024]{1,0:T(8,128)(2,1)S(1)}, bf16[512,1024]{1,0:T(8,128)(2,1)}, u32[]{:S(2)}) copy-start(bf16[512,1024]{1,0:T(8,128)(2,1)} %refs_2_.1) | copy-start | bytes 3145732
  0.0 17.2 %copy-start.8 = (bf16[1024,512]{1,0:T(8,128)(2,1)S(1)}, bf16[1024,512]{1,0:T(8,128)(2,1)}, u32[]{:S(2)}) copy-start(bf16[1024,512]{1,0:T(8,128)(2,1)} %refs_0_.2) | copy-start | bytes 3145732
  0.0 37.2 %collective-permute-start = (bf16[128,1024]{1,0:T(8,128)(2,1)}, bf16[128,1024]{1,0:T(8,128)(2,1)S(1)}, u32[]{:S(2)}, u32[]{:S(2)}) collective-permute-start(bf16[128,1024]{1,0:T(8,128)(2,1)} %refs_0_.1), channel_id=1, source_target_pairs={{0,1},{1,0},{2,3},{3,2},{4,5},{5,4},{6,7},{7,6},{8,9},{9,8},{10,11... | collective-permute-start | bytes 786440 | tf_op jit(solution)/shard_map/ppermute | solution.py:438
  11.0 19.2 %all-to-all-start = ((f16[32,4,1536]{2,1,0:T(4,128)(2,1)}), f16[32,4,1536]{2,1,0:T(4,128)(2,1)S(1)}, u32[]{:S(2)}, u32[]{:S(2)}) async-start(f16[32,4,1536]{2,1,0:T(4,128)(2,1)} %reshape.106), calls=%async_computation | async-start | bytes 786432 | tf_op jit(solution)/shard_map/all_to_all | solution.py:36
  17.2 4.8 %copy-start.10 = (s32[1,256]{1,0:T(1,128)S(1)}, s32[1,256]{1,0:T(1,128)}, u32[]{:S(2)}) copy-start(s32[1,256]{1,0:T(1,128)} %param.39) | copy-start | bytes 3076
  17.3 5.0 %copy-start.11 = (f32[256]{0:T(256)S(1)}, f32[256]{0:T(256)}, u32[]{:S(2)}) copy-start(f32[256]{0:T(256)} %param.23) | copy-start | bytes 3076
  17.3 5.0 %copy-start.12 = (f32[256]{0:T(256)S(1)}, f32[256]{0:T(256)}, u32[]{:S(2)}) copy-start(f32[256]{0:T(256)} %param.22) | copy-start | bytes 3076
  17.3 5.0 %copy-start.14 = (s32[16]{0:T(128)S(1)}, s32[16]{0:T(128)}, u32[]{:S(2)}) copy-start(s32[16]{0:T(128)} %param.36) | copy-start | bytes 196
  17.3 18.1 %copy-start.15 = (s32[2]{0:T(128)S(1)}, s32[2]{0:T(128)}, u32[]{:S(2)}) copy-start(s32[2]{0:T(128)} %param.37) | copy-start | bytes 28
  17.3 18.5 %copy-start.13 = (s32[16]{0:T(128)S(1)}, s32[16]{0:T(128)}, u32[]{:S(2)}) copy-start(s32[16]{0:T(128)} %param.38) | copy-start | bytes 196
  17.3 18.7 %copy-start.9 = (bf16[1,256,512]{2,1,0:T(8,128)(2,1)S(1)}, bf16[1,256,512]{2,1,0:T(8,128)(2,1)}, u32[]{:S(2)}) copy-start(bf16[1,256,512]{2,1,0:T(8,128)(2,1)} %param.34) | copy-start | bytes 786436
  20.2 41.7 %copy-start.1 = (bf16[128,1024]{1,0:T(8,128)(2,1)S(1)}, bf16[128,1024]{1,0:T(8,128)(2,1)}, u32[]{:S(2)}) copy-start(bf16[128,1024]{1,0:T(8,128)(2,1)} %refs_0_.1) | copy-start | bytes 786436
  20.2 72.5 %collective-permute-start.1 = (bf16[3072,512]{1,0:T(8,128)(2,1)}, bf16[3072,512]{1,0:T(8,128)(2,1)}, u32[]{:S(2)}, u32[]{:S(2)}) collective-permute-start(bf16[3072,512]{1,0:T(8,128)(2,1)} %pad_maximum_fusion), channel_id=1, source_target_pairs={{0,1},{1,0},{2,3},{3,2},{4,5},{5,4},{6,7},{7,6},{8,9},{9,8},{10,11... | collective-permute-start | bytes 9437192 | tf_op jit(solution)/shard_map/ppermute | solution.py:438
  22.0 55.4 %copy-start.2 = (s32[2]{0:T(128)}, s32[2]{0:T(128)S(1)}, u32[]{:S(2)}) copy-start(s32[2]{0:T(128)S(1)} %pad_add_fusion.where_ref) | copy-start | bytes 28
  31.8 13.5 %all-to-all-start.1 = ((bf16[16,4,2048]{2,1,0:T(4,128)(2,1)}), bf16[16,4,2048]{2,1,0:T(4,128)(2,1)S(1)}, u32[]{:S(2)}, u32[]{:S(2)}) async-start(bf16[16,4,2048]{2,1,0:T(4,128)(2,1)} %get-tuple-element.13), calls=%async_computation.1 | async-start | bytes 524288 | tf_op jit(solution)/shard_map/all_to_all | solution.py:36
  36.0 41.5 %copy-start.5 = (f32[2048]{0:T(1024)S(1)}, f32[2048]{0:T(1024)}, u32[]{:S(2)}) copy-start(f32[2048]{0:T(1024)} %param.24) | copy-start | bytes 24580
  36.0 41.5 %copy-start.6 = (f32[2048]{0:T(1024)S(1)}, f32[2048]{0:T(1024)}, u32[]{:S(2)}) copy-start(f32[2048]{0:T(1024)} %param.25) | copy-start | bytes 24580
  63.9 13.5 %all-to-all-start.3 = ((bf16[16,4,2048]{2,1,0:T(4,128)(2,1)}), bf16[16,4,2048]{2,1,0:T(4,128)(2,1)S(1)}, u32[]{:S(2)}, u32[]{:S(2)}) async-start(bf16[16,4,2048]{2,1,0:T(4,128)(2,1)} %combine_out.1), calls=%async_computation.3 | async-start | bytes 524288 | tf_op jit(solution)/shard_map/all_to_all | solution.py:36
  91.7 21.7 %copy-start.3 = (s32[2]{0:T(128)S(1)}, s32[2]{0:T(128)}, u32[]{:S(2)}) copy-start(s32[2]{0:T(128)} %copy-done.2) | copy-start | bytes 28
  91.7 21.7 %copy-start.4 = (f32[2048]{0:T(1024)S(1)}, f32[2048]{0:T(1024)}, u32[]{:S(2)}) copy-start(f32[2048]{0:T(1024)} %param.26) | copy-start | bytes 24580
where the time goes:
time: 128 us
  blocking collectives  60.5 us (47%)
  waiting for transfers between devices  26.3 us (21%)
  starting transfers between devices  17.9 us (14%)
  Pallas kernels  14.7 us (11%)
  other arithmetic  4.76 us (4%)
  local copies, waits for them, and re-layouts  2.94 us (2%)
    all_to_all x4, blocking collectives, exchange(): lax.all_to_all(blocks, axes, split_axis=0, concat_axis=0, tiled=True, axi...  55.4 us
    all_to_all x3, waiting for transfers between devices, exchange(): lax.all_to_all(blocks, axes, split_axis=0, concat_axis=0, tiled=True, axi...  25.2 us
    pallas_call x7, Pallas kernels, call(): pl.pallas_call(kernel, name=name, out_shape=out_shape, in_specs=in_specs,...  14.7 us
    all_to_all x3, starting transfers between devices, exchange(): lax.all_to_all(blocks, axes, split_axis=0, concat_axis=0, tiled=True, axi...  13.2 us
    all_gather x1, blocking collectives, on_device(): normed_all = lax.all_gather(normed_cols, 'req', axis=0, tiled=True)  5.1 us
    ppermute x2, starting transfers between devices, shifted(): lax.ppermute(values, 'req', [(i, (i + j) % req_count) for i in range(req_...  4.78 us
    concatenate x1, other arithmetic, on_device(): packed = shifted(jnp.concatenate([w_gate, w_up] + pieces))[1:]  2.86 us
  transfers between devices with their start and end apart: 5, of which 4 were waited for; matrix products, arithmetic and copies ran while one was open for 6% of the time, Pallas kernels for 7%

commit v1 on v0

--- a/solution.py
+++ b/solution.py
@@ -223,54 +223,73 @@
         out_ref[i] = layer
 
 
-def ffn_kernel(req_count, where_ref, x_ref, *refs):
-    count = req_count + 2
-    w_refs, out_ref, x_held, parts_ref = refs[:count], *refs[count : count + 3]
-    held, sem_ref = refs[count + 3 : -1], refs[-1]
-    gate_rows, width = w_refs[0].shape
-    down_rows, down_width = w_refs[2].shape
-    load_x = pltpu.make_async_copy(x_ref, x_held, sem_ref.at[3 * req_count])
-    load_x.start()
-    x_ref = x_held
-    copies = []
-
-    def load(source, target):
-        copies.append(pltpu.make_async_copy(source, target, sem_ref.at[len(copies)]))
-        copies[-1].start()
-
-    for i in range(3):
-        load(w_refs[i], held[i])
-    packed_rows = 2 * gate_rows + down_rows * (down_width // width)
+def start_copies(moves, sem_ref):
+    copies = [
+        pltpu.make_async_copy(source, target, sem_ref.at[i])
+        for i, (source, target) in enumerate(moves)
+    ]
+    for copy in copies:
+        copy.start()
+    return copies
+
+
+def own_kernel(req_count, where_ref, x_ref, gate_ref, up_ref, out_ref, x_held, held, sem_ref):
+    copies = start_copies(
+        [(x_ref, x_held), (gate_ref, held.at[0]), (up_ref, held.at[1])], sem_ref
+    )
+    rows = gate_ref.shape[0]
+    blocks, steps, _ = x_held.shape
+    copies[0].wait()
+    start = where_ref[1] * rows
+    part = x_held[:, :, pl.ds(pl.multiple_of(start, rows), rows)].reshape(blocks * steps, rows)
+    for i in range(2):
+        copies[i + 1].wait()
+        out_ref[i] = jnp.dot(part, held[i], preferred_element_type=jnp.float32)
+
+
+def ffn_kernel(req_count, gate_rows, where_ref, x_ref, own_ref, down_ref, *refs):
+    others = req_count - 1
+    packed_refs = refs[:others]
+    out_ref, x_held, own_held, down_held, parts_ref = refs[others : others + 5]
+    held, sem_ref = refs[others + 5 : -1], refs[-1]
+    down_rows, down_width = down_ref.shape
+    packed_rows, width = packed_refs[0].shape
+    moves = [(x_ref, x_held), (own_ref, own_held)]
     spans = [(0, gate_rows), (gate_rows, gate_rows), (2 * gate_rows, packed_rows - 2 * gate_rows)]
-    for j in range(3, count):
+    for j in range(others):
         for first, rows in spans:
-            load(w_refs[j].at[pl.ds(first, rows), :], held[j].at[pl.ds(first, rows), :])
-    blocks, steps, _ = x_ref.shape
+            span = pl.ds(first, rows)
+            moves.append((packed_refs[j].at[span, :], held[j].at[span, :]))
+    moves.append((down_ref, down_held))
+    copies = start_copies(moves, sem_ref)
+    blocks, steps, _ = x_held.shape
     tokens = blocks * steps
-    load_x.wait()
-    gate_out = up_out = None
-    for j in range(req_count):
-        first = lax.rem(where_ref[1] - j + req_count, req_count) * gate_rows
-        cols = pl.ds(pl.multiple_of(first, gate_rows), gate_rows)
-        part = x_ref[:, :, cols].reshape(tokens, gate_rows)
-        copies[3 * j].wait()
-        gate_w = held[0][...] if j == 0 else held[j + 2][:gate_rows, :]
-        gate = jnp.dot(part, gate_w, preferred_element_type=jnp.float32)
-        copies[3 * j + 1].wait()
-        up_w = held[1][...] if j == 0 else held[j + 2][gate_rows : 2 * gate_rows, :]
-        up = jnp.dot(part, up_w, preferred_element_type=jnp.float32)
-        gate_out = gate if j == 0 else gate_out + gate
-        up_out = up if j == 0 else up_out + up
+    copies[0].wait()
+    gates, ups = [], []
+    for j in range(others):
+        start = lax.rem(where_ref[1] - j - 1 + req_count, req_count) * gate_rows
+        part = x_held[:, :, pl.ds(pl.multiple_of(start, gate_rows), gate_rows)]
+        part = part.reshape(tokens, gate_rows)
+        copies[3 * j + 2].wait()
+        gates.append(jnp.dot(part, held[j][:gate_rows, :], preferred_element_type=jnp.float32))
+        copies[3 * j + 3].wait()
+        up_w = held[j][gate_rows : 2 * gate_rows, :]
+        ups.append(jnp.dot(part, up_w, preferred_element_type=jnp.float32))
+    copies[1].wait()
+    gate_out, up_out = own_held[0], own_held[1]
+    for gate, up in zip(gates, ups):
+        gate_out = gate_out + gate
+        up_out = up_out + up
     activated = (jax.nn.gelu(gate_out, approximate=True) * up_out).astype(jnp.bfloat16)
     sends = []
     for j in range(req_count):
-        copies[3 * j + 2].wait()
+        copies[-1 if j == 0 else 3 * j + 1].wait()
         for piece in range(down_width // width):
             if j == 0:
-                down_w = held[2][:, piece * width : (piece + 1) * width]
+                down_w = down_held[:, piece * width : (piece + 1) * width]
             else:
                 row = 2 * gate_rows + piece * down_rows
-                down_w = held[j + 2][row : row + down_rows, :]
+                down_w = held[j - 1][row : row + down_rows, :]
             part = jnp.dot(activated, down_w, preferred_element_type=jnp.float32)
             part = part.astype(jnp.bfloat16)
             index = j * (down_width // width) + piece
@@ -280,7 +299,7 @@
                 pltpu.make_async_copy(
                     parts_ref.at[index],
                     out_ref.at[:, :, pl.ds(index * width, width)],
-                    sem_ref.at[3 * req_count + 1 + index],
+                    sem_ref.at[len(copies) + index],
                 )
             )
             sends[-1].start()
@@ -544,20 +563,41 @@
         post_attn_gain.reshape(1, D),
         ffn_gain.reshape(1, D),
     )
-    held = [w_gate, w_up, w_down] + list(packed)
+    ffn_in = exchange(ffn_blocks, "seq")
+    x_space = pltpu.VMEM((seq_count, share, D), jnp.bfloat16)
+    own_part = call(
+        functools.partial(own_kernel, req_count),
+        "own_gate_up",
+        jax.ShapeDtypeStruct((2, tokens, width), jnp.float32),
+        where,
+        ffn_in,
+        w_gate,
+        w_up,
+        scratch=[
+            x_space,
+            pltpu.VMEM((2,) + w_gate.shape, jnp.bfloat16),
+            pltpu.SemaphoreType.DMA((3,)),
+        ],
+        hbm_from=1,
+        limit=56,
+    )
     down_part = call(
-        functools.partial(ffn_kernel, req_count),
+        functools.partial(ffn_kernel, req_count, w_gate.shape[0]),
         "feed_forward",
         jax.ShapeDtypeStruct((seq_count, share, D), jnp.bfloat16),
         where,
-        exchange(ffn_blocks, "seq"),
-        *held,
+        ffn_in,
+        own_part,
+        w_down,
+        *packed,
         scratch=[
-            pltpu.VMEM((seq_count, share, D), jnp.bfloat16),
+            x_space,
+            pltpu.VMEM((2, tokens, width), jnp.float32),
+            pltpu.VMEM(w_down.shape, jnp.bfloat16),
             pltpu.VMEM((D // width, seq_count, share, width), jnp.bfloat16),
         ]
-        + [pltpu.VMEM(w.shape, w.dtype) for w in held]
-        + [pltpu.SemaphoreType.DMA((3 * req_count + 1 + D // width,))],
+        + [pltpu.VMEM(w.shape, w.dtype) for w in packed]
+        + [pltpu.SemaphoreType.DMA((3 * req_count + D // width,))],
         hbm_from=1,
         out_space=pltpu.HBM,
         limit=56,

time: 128 us -> 128 us (level)
  Pallas kernels: 14.7 us -> 17.2 us
  blocking collectives: 60.5 us -> 58.7 us
    pallas_call x7 -> x8, Pallas kernels: 14.7 us -> 17.2 us  [call(): pl.pallas_call(kernel, name=name, out_shape=out_shape, in_specs=in_specs,...]
    all_to_all x4, blocking collectives: 55.4 us -> 53.5 us  [exchange(): lax.all_to_all(blocks, axes, split_axis=0, concat_axis=0, tiled=True, axi...]
  transfers between devices with their start and end apart: 5 -> 5, of which waited for: 4 -> 3; matrix products, arithmetic and copies ran while one was open for 6% -> 6% of each run, Pallas kernels for 7% -> 9%
where the time goes in v1:
time: 128 us; the launch traced here: 127 us
  blocking collectives  58.7 us (46%)
  waiting for transfers between devices  25.2 us (20%)
  starting transfers between devices  17.9 us (14%)
  Pallas kernels  17.2 us (13%)
  other arithmetic  4.81 us (4%)
  local copies, waits for them, and re-layouts  2.95 us (2%)
    all_to_all x4, blocking collectives, exchange(): lax.all_to_all(blocks, axes, split_axis=0, concat_axis=0, tiled=True, axi...  53.5 us
    all_to_all x3, waiting for transfers between devices, exchange(): lax.all_to_all(blocks, axes, split_axis=0, concat_axis=0, tiled=True, axi...  25.2 us
    pallas_call x8, Pallas kernels, call(): pl.pallas_call(kernel, name=name, out_shape=out_shape, in_specs=in_specs,...  17.2 us
    all_to_all x3, starting transfers between devices, exchange(): lax.all_to_all(blocks, axes, split_axis=0, concat_axis=0, tiled=True, axi...  13.2 us
    all_gather x1, blocking collectives, on_device(): normed_all = lax.all_gather(normed_cols, 'req', axis=0, tiled=True)  5.1 us
    ppermute x2, starting transfers between devices, shifted(): lax.ppermute(values, 'req', [(i, (i + j) % req_count) for i in range(req_...  4.78 us
    concatenate x1, other arithmetic, on_device(): packed = shifted(jnp.concatenate([w_gate, w_up] + pieces))[1:]  2.92 us
  transfers between devices with their start and end apart: 5, of which 3 were waited for; matrix products, arithmetic and copies ran while one was open for 6% of the time, Pallas kernels for 9%

profile of v1, /device:TPU:0, one launch (start us, length us, event | category | flops | bytes accessed | tf_op | source)
XLA Modules:
  0.0 127.3 jit_solution(12720497155030607748)
XLA Ops:
  0.0 0.0 copy-start
  0.0 3.0 %collective-permute-start = (bf16[128,1024]{1,0:T(8,128)(2,1)}, bf16[128,1024]{1,0:T(8,128)(2,1)S(1)}, u32[]{:S(2)}, u32[]{:S(2)}) collective-permute-start(bf16[128,1024]{1,0:T(8,128)(2,1)} %refs_0_), channel_id=1, source_target_pairs={{0,1},{1,0},{2,3},{3,2},{4,5},{5,4},{6,7},{7,6},{8,9},{9,8},{10,11... | collective-permute-start | bytes 786440 | tf_op jit(solution)/shard_map/ppermute | solution.py:457
  3.0 1.8 %norm_columns.1 = bf16[64,128]{1,0:T(8,128)(2,1)} custom-call(s32[1]{0:T(128)} %bitcast.where_ref, bf16[16,4,2048]{2,1,0:T(4,128)(2,1)} %hidden_ref.1, f32[1,2048]{1,0:T(1,128)} %bitcast.34), custom_call_target="tpu_custom_call" | custom-call | tf_op jit(solution)/shard_map/norm_columns/pallas_call | solution.py:60
  4.8 5.1 %all_gather.3 = bf16[128,128]{1,0:T(8,128)(2,1)S(1)} all-gather(bf16[64,128]{1,0:T(8,128)(2,1)} %norm_columns.1), channel_id=1, replica_groups=mesh['seq'=16,'req'=2] {'req'}, dimensions={0}, use_global_device_ids=true | all-gather | bytes 49152 | tf_op jit(solution)/shard_map/all_gather | solution.py:478
  9.9 0.0 copy-done
  9.9 0.3 fusion
  10.1 0.9 reshape.106
  11.0 6.1 %all-to-all-start = ((f16[32,4,1536]{2,1,0:T(4,128)(2,1)}), f16[32,4,1536]{2,1,0:T(4,128)(2,1)S(1)}, u32[]{:S(2)}, u32[]{:S(2)}) async-start(f16[32,4,1536]{2,1,0:T(4,128)(2,1)} %reshape.106), calls=%async_computation | async-start | bytes 786432 | tf_op jit(solution)/shard_map/all_to_all | solution.py:36
  17.1 0.0 copy-done.7
  17.2 0.1 fusion.4
  17.2 0.0 copy-done.8
  17.2 0.0 copy-start.10
  17.3 0.0 copy-start.11
  17.3 0.0 copy-start.12
  17.3 0.0 copy-start.14
  17.3 0.0 copy-start.15
  17.3 0.0 copy-start.13
  17.3 0.0 copy-start.9
  17.3 2.9 %pad_maximum_fusion = bf16[3072,512]{1,0:T(8,128)(2,1)} fusion(bf16[512,512]{1,0:T(8,128)(2,1)S(1)} %get-tuple-element.22, bf16[512,512]{1,0:T(8,128)(2,1)S(1)} %get-tuple-element.21, bf16[1024,512]{1,0:T(8,128)(2,1)} %up_ref.1, bf16[1024,512]{1,0:T(8,128)(2,1)S(1)} %copy-done.8), kind=kLoop, calls=%fused_computation | loop fusion | flops 12582912 | bytes 6291456 | tf_op jit(solution)/shard_map/concatenate | solution.py:482
  20.2 1.8 %collective-permute-start.1 = (bf16[3072,512]{1,0:T(8,128)(2,1)}, bf16[3072,512]{1,0:T(8,128)(2,1)}, u32[]{:S(2)}, u32[]{:S(2)}) collective-permute-start(bf16[3072,512]{1,0:T(8,128)(2,1)} %pad_maximum_fusion), channel_id=1, source_target_pairs={{0,1},{1,0},{2,3},{3,2},{4,5},{5,4},{6,7},{7,6},{8,9},{9,8},{10,11... | collective-permute-start | bytes 9437192 | tf_op jit(solution)/shard_map/ppermute | solution.py:457
  22.0 0.1 pad_add_fusion.where_ref
  22.1 0.0 copy-done.10
  22.1 0.2 select_reduce_fusion
  22.3 0.0 copy-done.11
  22.3 0.0 copy-done.12
  22.3 0.0 copy-done.14
  22.4 0.1 iota_compare_fusion.1
  22.4 0.1 iota_add_fusion
  22.5 7.7 %all-to-all-done = f16[32,4,1536]{2,1,0:T(4,128)(2,1)S(1)} async-done(((f16[32,4,1536]{2,1,0:T(4,128)(2,1)}), f16[32,4,1536]{2,1,0:T(4,128)(2,1)S(1)}, u32[]{:S(2)}, u32[]{:S(2)}) %all-to-all-start) | async-done | bytes 393248 | tf_op jit(solution)/shard_map/all_to_all | solution.py:36
  30.3 0.2 convert_reduce_fusion
  30.4 1.4 %head_norm.1 = (bf16[16,4,2048]{2,1,0:T(4,128)(2,1)}, f32[8,512]{1,0:T(8,128)S(1)}, f32[8,512]{1,0:T(8,128)S(1)}) custom-call(s32[2]{0:T(128)S(1)} %pad_add_fusion.where_ref, f32[2,4,1536]{2,1,0:T(4,128)S(1)} %broadcast_multiply_fusion.projected_ref, f32[2,256]{1,0:T(2,128)S(1)} %pad_maximum_fusion.3.gains_ref), custom_call_target="tpu_custom_call" | custom-call | tf_op jit(solution)/shard_map/head_norm/pallas_call | solution.py:60
  31.8 3.5 %all-to-all-start.1 = ((bf16[16,4,2048]{2,1,0:T(4,128)(2,1)}), bf16[16,4,2048]{2,1,0:T(4,128)(2,1)S(1)}, u32[]{:S(2)}, u32[]{:S(2)}) async-start(bf16[16,4,2048]{2,1,0:T(4,128)(2,1)} %get-tuple-element.13), calls=%async_computation.1 | async-start | bytes 524288 | tf_op jit(solution)/shard_map/all_to_all | solution.py:36
  35.4 0.0 copy-done.15
  35.4 0.1 lt.51
  35.5 0.1 broadcast_in_dim.20
  35.5 0.1 eq.57
  35.6 0.1 add.52
  35.7 0.1 and.36
  35.8 0.0 copy-done.13
  35.8 0.1 fusion.1
  36.0 0.0 copy-start.5
  36.0 0.0 copy-start.6
  36.0 0.0 copy-done.9
  36.0 1.2 pad_maximum_fusion.1
  37.2 0.0 collective-permute-done.refs_1_
  37.2 8.2 %all-to-all-done.1.q_ref = bf16[16,4,2048]{2,1,0:T(4,128)(2,1)S(1)} async-done(((bf16[16,4,2048]{2,1,0:T(4,128)(2,1)}), bf16[16,4,2048]{2,1,0:T(4,128)(2,1)S(1)}, u32[]{:S(2)}, u32[]{:S(2)}) %all-to-all-start.1) | async-done | bytes 262176 | tf_op jit(solution)/shard_map/all_to_all | solution.py:36
  45.4 2.6 %block_attention.1 = bf16[16,80,128]{2,1,0:T(8,128)(2,1)S(1)} custom-call(s32[2]{0:T(128)S(1)} %pad_add_fusion.where_ref, bf16[16,4,2048]{2,1,0:T(4,128)(2,1)S(1)} %all-to-all-done.1.q_ref, f32[64,512]{1,0:T(8,128)S(1)} %reshape.107.live_ref, f32[8,512]{1,0:T(8,128)S(1)} %get-tuple-element.15.new_k_ref, f32[8,512]{1,0:T(8,128)S(1)} %get-tuple-element.16.new_v_ref, ...), custom_call_target="tpu_custom_call" | custom-call | tf_op jit(solution)/shard_map/block_attention/pallas_call | solution.py:60
  48.0 13.9 %all_to_all.35.got_ref = bf16[16,80,128]{2,1,0:T(8,128)(2,1)S(1)} all-to-all(bf16[16,80,128]{2,1,0:T(8,128)(2,1)S(1)} %block_attention.1), channel_id=1, replica_groups=mesh['seq'=16,'req'=2] {'seq'}, dimensions={0} | all-to-all | bytes 655360 | tf_op jit(solution)/shard_map/all_to_all | solution.py:36
  61.9 2.0 %combine_out.1 = bf16[16,4,2048]{2,1,0:T(4,128)(2,1)} custom-call(s32[2]{0:T(128)S(1)} %pad_add_fusion.where_ref, bf16[16,80,128]{2,1,0:T(8,128)(2,1)S(1)} %all_to_all.35.got_ref, bf16[128,1024]{1,0:T(8,128)(2,1)S(1)} %copy-done.1, bf16[128,1024]{1,0:T(8,128)(2,1)S(1)} %collective-permute-done.refs_1_), custom_call_target="tpu_custom_call" | custom-call | tf_op jit(solution)/shard_map/combine_out/pallas_call | solution.py:60
  63.9 3.5 %all-to-all-start.3 = ((bf16[16,4,2048]{2,1,0:T(4,128)(2,1)}), bf16[16,4,2048]{2,1,0:T(4,128)(2,1)S(1)}, u32[]{:S(2)}, u32[]{:S(2)}) async-start(bf16[16,4,2048]{2,1,0:T(4,128)(2,1)} %combine_out.1), calls=%async_computation.3 | async-start | bytes 524288 | tf_op jit(solution)/shard_map/all_to_all | solution.py:36
  67.5 0.7 dynamic-slice_bitcast_fusion.hidden_ref
  68.2 9.3 %all-to-all-done.3.got_ref = bf16[16,4,2048]{2,1,0:T(4,128)(2,1)S(1)} async-done(((bf16[16,4,2048]{2,1,0:T(4,128)(2,1)}), bf16[16,4,2048]{2,1,0:T(4,128)(2,1)S(1)}, u32[]{:S(2)}, u32[]{:S(2)}) %all-to-all-start.3) | async-done | bytes 262176 | tf_op jit(solution)/shard_map/all_to_all | solution.py:36
  77.5 0.0 copy-done.5
  77.5 0.9 residual_norms.1
  78.4 13.3 %all_to_all.36.x_ref = bf16[16,4,2048]{2,1,0:T(4,128)(2,1)} all-to-all(bf16[16,4,2048]{2,1,0:T(4,128)(2,1)S(1)} %get-tuple-element.19), channel_id=1, replica_groups=mesh['seq'=16,'req'=2] {'seq'}, dimensions={0} | all-to-all | bytes 524288 | tf_op jit(solution)/shard_map/all_to_all | solution.py:36
  91.7 3.3 %own_gate_up.1.own_ref = f32[2,64,512]{2,1,0:T(8,128)} custom-call(s32[2]{0:T(128)} %copy-done.2, bf16[16,4,2048]{2,1,0:T(4,128)(2,1)} %all_to_all.36.x_ref, bf16[1024,512]{1,0:T(8,128)(2,1)} %gate_ref.1, bf16[1024,512]{1,0:T(8,128)(2,1)} %up_ref.1), custom_call_target="tpu_custom_call" | custom-call | tf_op jit(solution)/shard_map/own_gate_up/pallas_call | solution.py:60
  95.0 0.0 copy-start.4
  95.0 0.0 collective-permute-done.1.refs_0_
  95.0 4.4 %feed_forward.1 = bf16[16,4,2048]{2,1,0:T(4,128)(2,1)} custom-call(s32[2]{0:T(128)} %copy-done.2, bf16[16,4,2048]{2,1,0:T(4,128)(2,1)} %all_to_all.36.x_ref, f32[2,64,512]{2,1,0:T(8,128)} %own_gate_up.1.own_ref, bf16[512,1024]{1,0:T(8,128)(2,1)} %down_ref.1, bf16[3072,512]{1,0:T(8,128)(2,1)} %collective-permute-done.1.refs_0_), custom_call_target="tpu_custom_call" | custom-call | tf_op jit(solution)/shard_map/feed_forward/pallas_call | solution.py:60
  99.4 13.5 %all_to_all.37.got_ref = bf16[16,4,2048]{2,1,0:T(4,128)(2,1)S(1)} all-to-all(bf16[16,4,2048]{2,1,0:T(4,128)(2,1)} %feed_forward.1), channel_id=1, replica_groups=mesh['seq'=16,'req'=2] {'seq'}, dimensions={0} | all-to-all | bytes 524288 | tf_op jit(solution)/shard_map/all_to_all | solution.py:36
  112.9 0.0 copy-done.4
  112.9 0.8 last_norm.1
  113.7 12.8 %all_to_all.38 = bf16[16,4,2048]{2,1,0:T(4,128)(2,1)S(1)} all-to-all(bf16[16,4,2048]{2,1,0:T(4,128)(2,1)S(1)} %last_norm.1), channel_id=1, replica_groups=mesh['seq'=16,'req'=2] {'seq'}, dimensions={0} | all-to-all | bytes 524288 | tf_op jit(solution)/shard_map/all_to_all | solution.py:36
  126.6 0.7 copy.24
  (19 shorter events, 0.2 us)
Async XLA Ops:
  0.0 9.9 %copy-start = (bf16[128,1536]{1,0:T(8,128)(2,1)S(1)}, bf16[128,1536]{1,0:T(8,128)(2,1)}, u32[]{:S(2)}) copy-start(bf16[128,1536]{1,0:T(8,128)(2,1)} %param.27) | copy-start | bytes 1179652
  0.0 17.1 %copy-start.7 = (bf16[512,1024]{1,0:T(8,128)(2,1)S(1)}, bf16[512,1024]{1,0:T(8,128)(2,1)}, u32[]{:S(2)}) copy-start(bf16[512,1024]{1,0:T(8,128)(2,1)} %down_ref.1) | copy-start | bytes 3145732
  0.0 17.2 %copy-start.8 = (bf16[1024,512]{1,0:T(8,128)(2,1)S(1)}, bf16[1024,512]{1,0:T(8,128)(2,1)}, u32[]{:S(2)}) copy-start(bf16[1024,512]{1,0:T(8,128)(2,1)} %gate_ref.1) | copy-start | bytes 3145732
  0.0 37.2 %collective-permute-start = (bf16[128,1024]{1,0:T(8,128)(2,1)}, bf16[128,1024]{1,0:T(8,128)(2,1)S(1)}, u32[]{:S(2)}, u32[]{:S(2)}) collective-permute-start(bf16[128,1024]{1,0:T(8,128)(2,1)} %refs_0_), channel_id=1, source_target_pairs={{0,1},{1,0},{2,3},{3,2},{4,5},{5,4},{6,7},{7,6},{8,9},{9,8},{10,11... | collective-permute-start | bytes 786440 | tf_op jit(solution)/shard_map/ppermute | solution.py:457
  11.0 19.2 %all-to-all-start = ((f16[32,4,1536]{2,1,0:T(4,128)(2,1)}), f16[32,4,1536]{2,1,0:T(4,128)(2,1)S(1)}, u32[]{:S(2)}, u32[]{:S(2)}) async-start(f16[32,4,1536]{2,1,0:T(4,128)(2,1)} %reshape.106), calls=%async_computation | async-start | bytes 786432 | tf_op jit(solution)/shard_map/all_to_all | solution.py:36
  17.2 4.9 %copy-start.10 = (s32[1,256]{1,0:T(1,128)S(1)}, s32[1,256]{1,0:T(1,128)}, u32[]{:S(2)}) copy-start(s32[1,256]{1,0:T(1,128)} %param.39) | copy-start | bytes 3076
  17.3 5.0 %copy-start.11 = (f32[256]{0:T(256)S(1)}, f32[256]{0:T(256)}, u32[]{:S(2)}) copy-start(f32[256]{0:T(256)} %param.23) | copy-start | bytes 3076
  17.3 5.0 %copy-start.12 = (f32[256]{0:T(256)S(1)}, f32[256]{0:T(256)}, u32[]{:S(2)}) copy-start(f32[256]{0:T(256)} %param.22) | copy-start | bytes 3076
  17.3 5.1 %copy-start.14 = (s32[16]{0:T(128)S(1)}, s32[16]{0:T(128)}, u32[]{:S(2)}) copy-start(s32[16]{0:T(128)} %param.36) | copy-start | bytes 196
  17.3 18.1 %copy-start.15 = (s32[2]{0:T(128)S(1)}, s32[2]{0:T(128)}, u32[]{:S(2)}) copy-start(s32[2]{0:T(128)} %param.37) | copy-start | bytes 28
  17.3 18.5 %copy-start.13 = (s32[16]{0:T(128)S(1)}, s32[16]{0:T(128)}, u32[]{:S(2)}) copy-start(s32[16]{0:T(128)} %param.38) | copy-start | bytes 196
  17.3 18.7 %copy-start.9 = (bf16[1,256,512]{2,1,0:T(8,128)(2,1)S(1)}, bf16[1,256,512]{2,1,0:T(8,128)(2,1)}, u32[]{:S(2)}) copy-start(bf16[1,256,512]{2,1,0:T(8,128)(2,1)} %param.34) | copy-start | bytes 786436
  20.2 41.6 %copy-start.1 = (bf16[128,1024]{1,0:T(8,128)(2,1)S(1)}, bf16[128,1024]{1,0:T(8,128)(2,1)}, u32[]{:S(2)}) copy-start(bf16[128,1024]{1,0:T(8,128)(2,1)} %refs_0_) | copy-start | bytes 786436
  20.2 74.8 %collective-permute-start.1 = (bf16[3072,512]{1,0:T(8,128)(2,1)}, bf16[3072,512]{1,0:T(8,128)(2,1)}, u32[]{:S(2)}, u32[]{:S(2)}) collective-permute-start(bf16[3072,512]{1,0:T(8,128)(2,1)} %pad_maximum_fusion), channel_id=1, source_target_pairs={{0,1},{1,0},{2,3},{3,2},{4,5},{5,4},{6,7},{7,6},{8,9},{9,8},{10,11... | collective-permute-start | bytes 9437192 | tf_op jit(solution)/shard_map/ppermute | solution.py:457
  22.1 55.4 %copy-start.2 = (s32[2]{0:T(128)}, s32[2]{0:T(128)S(1)}, u32[]{:S(2)}) copy-start(s32[2]{0:T(128)S(1)} %pad_add_fusion.where_ref) | copy-start | bytes 28
  31.8 13.5 %all-to-all-start.1 = ((bf16[16,4,2048]{2,1,0:T(4,128)(2,1)}), bf16[16,4,2048]{2,1,0:T(4,128)(2,1)S(1)}, u32[]{:S(2)}, u32[]{:S(2)}) async-start(bf16[16,4,2048]{2,1,0:T(4,128)(2,1)} %get-tuple-element.13), calls=%async_computation.1 | async-start | bytes 524288 | tf_op jit(solution)/shard_map/all_to_all | solution.py:36
  36.0 41.5 %copy-start.5 = (f32[2048]{0:T(1024)S(1)}, f32[2048]{0:T(1024)}, u32[]{:S(2)}) copy-start(f32[2048]{0:T(1024)} %param.24) | copy-start | bytes 24580
  36.0 41.5 %copy-start.6 = (f32[2048]{0:T(1024)S(1)}, f32[2048]{0:T(1024)}, u32[]{:S(2)}) copy-start(f32[2048]{0:T(1024)} %param.25) | copy-start | bytes 24580
  63.9 13.5 %all-to-all-start.3 = ((bf16[16,4,2048]{2,1,0:T(4,128)(2,1)}), bf16[16,4,2048]{2,1,0:T(4,128)(2,1)S(1)}, u32[]{:S(2)}, u32[]{:S(2)}) async-start(bf16[16,4,2048]{2,1,0:T(4,128)(2,1)} %combine_out.1), calls=%async_computation.3 | async-start | bytes 524288 | tf_op jit(solution)/shard_map/all_to_all | solution.py:36
  95.0 18.0 %copy-start.3 = (s32[2]{0:T(128)S(1)}, s32[2]{0:T(128)}, u32[]{:S(2)}) copy-start(s32[2]{0:T(128)} %copy-done.2) | copy-start | bytes 28
  95.0 17.9 %copy-start.4 = (f32[2048]{0:T(1024)S(1)}, f32[2048]{0:T(1024)}, u32[]{:S(2)}) copy-start(f32[2048]{0:T(1024)} %param.26) | copy-start | bytes 24580
